TPU v7x, 256 devices: a whole 4x4x8 slice. The times are simulated.
256 devices in a mesh: row: 16 (over z_lo, x, core), col: 16 (over z_hi, y).
Axes of the slice: x: 4, y: 4, z: 8 (z_hi: 4, z_lo: 2; z = z_hi * 2 + z_lo), core: 2. Of those that a mesh axis runs over, the one named last changes fastest.
Arguments:
- pair_input: bfloat16 [384, 384, 128], P('row', 'col'), may hold values from -6 to 6
- norm_mean: float32 [384, 384], P('row', 'col'), may hold values from -0.5 to 0.5
- norm_scale: float32 [384, 384], P('row', 'col'), may hold values from 0.5 to 2
- pair_mask: int32 [384, 384], P('row', 'col'), may hold values 0 or 1
- cotangent: bfloat16 [384, 384, 128], P('row', 'col'), may hold values from -6 to 6
- left_gate: bfloat16 [128, 128], replicated, may hold values from -0.5 to 0.5
- left_value: bfloat16 [128, 128], replicated, may hold values from -0.5 to 0.5
- right_gate: bfloat16 [128, 128], replicated, may hold values from -0.5 to 0.5
- right_value: bfloat16 [128, 128], replicated, may hold values from -0.5 to 0.5
- output_gate: bfloat16 [128, 128], replicated, may hold values from -0.5 to 0.5
- output_weight: bfloat16 [128, 128], replicated, may hold values from -0.5 to 0.5
Outputs:
- pair_grad: float32 [384, 384, 128], P('row', 'col')
Inputs may be any that keep to these rules, and one draw needn't show every extreme that they name: `pair_mask`: 1 marks a pair that takes part.
All inputs are finite; a program needn't handle non-finite values. No bound on the sum of `pair_mask` on one device may be relied on, other than what follows from the above.
Results may differ from a plain program's by a relative error of at most 0.0072.
Values may be sent and summed in bfloat16 or wider, within the bound.
No kernel may reach another device: no remote copies, remote signals or barrier semaphores. Data moves between devices by JAX's collectives and lax.ppermute only.
A program may use at most 128 MiB of HBM per device.

v0:
```python
import jax
import jax.numpy as jnp
from jax import lax
from jax.sharding import PartitionSpec as P

epsilon = 1e-05


def layer_back(grad, normed, scale):
    centre = jnp.mean(grad, axis=-1, keepdims=True)
    along = jnp.mean(grad * normed, axis=-1, keepdims=True)
    return scale * (grad - centre - normed * along)


def column_panel(right_edge):
    return lax.all_gather(right_edge, "row", axis=0, tiled=True)


def panel_right(right_edge):
    right_cols = column_panel(right_edge)
    return lax.all_to_all(right_cols, "col", split_axis=0, concat_axis=1, tiled=True)


def panel_grad_right(grad_mix, left_rows):
    partial_right = jnp.einsum(
        "ijh,ikh->jkh", grad_mix, left_rows, preferred_element_type=jnp.float32
    )
    moved_right = lax.all_to_all(partial_right, "col", split_axis=1, concat_axis=0, tiled=True)
    return lax.psum_scatter(moved_right, "row", scatter_dimension=0, tiled=True)


def per_device(
    pair_input,
    norm_mean,
    norm_scale,
    pair_mask,
    cotangent,
    left_gate,
    left_value,
    right_gate,
    right_value,
    output_gate,
    output_weight,
):
    rows_here, cols_here, width = pair_input.shape
    hidden = left_gate.shape[1]
    flat_rows = rows_here * cols_here
    normed = (pair_input.astype(jnp.float32) - norm_mean[:, :, None]) * norm_scale[:, :, None]
    normed_low = normed.astype(jnp.bfloat16)
    stacked = jnp.concatenate([left_gate, left_value, right_gate, right_value, output_gate], axis=1)
    projected = jnp.dot(
        normed_low.reshape(flat_rows, width), stacked, preferred_element_type=jnp.float32
    )
    keep = pair_mask.reshape(flat_rows, 1).astype(jnp.float32)
    left_sig = jax.nn.sigmoid(projected[:, :hidden])
    left_lin = projected[:, hidden : 2 * hidden]
    right_sig = jax.nn.sigmoid(projected[:, 2 * hidden : 3 * hidden])
    right_lin = projected[:, 3 * hidden : 4 * hidden]
    out_sig = jax.nn.sigmoid(projected[:, 4 * hidden :])
    left_edge = (
        (left_sig * left_lin * keep).astype(jnp.bfloat16).reshape(rows_here, cols_here, hidden)
    )
    right_edge = (
        (right_sig * right_lin * keep).astype(jnp.bfloat16).reshape(rows_here, cols_here, hidden)
    )
    left_rows = lax.all_gather(left_edge, "col", axis=1, tiled=True)
    right_mine = panel_right(right_edge)
    mixed = jnp.einsum("ikh,jkh->ijh", left_rows, right_mine, preferred_element_type=jnp.float32)
    centred = mixed - jnp.mean(mixed, axis=-1, keepdims=True)
    mix_scale = lax.rsqrt(jnp.mean(centred * centred, axis=-1, keepdims=True) + epsilon)
    mix_normed = centred * mix_scale
    out_lin = jnp.dot(
        mix_normed.astype(jnp.bfloat16).reshape(flat_rows, hidden),
        output_weight,
        preferred_element_type=jnp.float32,
    )
    upstream = cotangent.reshape(flat_rows, width).astype(jnp.float32)
    grad_y = (upstream * out_sig).astype(jnp.bfloat16)
    grad_gate = upstream * out_lin * out_sig * (1.0 - out_sig)
    grad_mixnorm = jnp.dot(grad_y, output_weight.T, preferred_element_type=jnp.float32).reshape(
        rows_here, cols_here, hidden
    )
    grad_mix = layer_back(grad_mixnorm, mix_normed, mix_scale).astype(jnp.bfloat16)
    partial_left = jnp.einsum(
        "ijh,jkh->ikh", grad_mix, right_mine, preferred_element_type=jnp.float32
    )
    grad_left = lax.psum_scatter(partial_left, "col", scatter_dimension=1, tiled=True)
    grad_right = panel_grad_right(grad_mix, left_rows)
    grad_left = grad_left.reshape(flat_rows, hidden) * keep
    grad_right = grad_right.reshape(flat_rows, hidden) * keep
    pre_grads = jnp.concatenate(
        [
            grad_left * left_lin * left_sig * (1.0 - left_sig),
            grad_left * left_sig,
            grad_right * right_lin * right_sig * (1.0 - right_sig),
            grad_right * right_sig,
            grad_gate,
        ],
        axis=1,
    ).astype(jnp.bfloat16)
    grad_normed = jnp.dot(pre_grads, stacked.T, preferred_element_type=jnp.float32).reshape(
        rows_here, cols_here, width
    )
    return layer_back(grad_normed, normed, norm_scale[:, :, None])


def solution(mesh):
    placed = (
        P("row", "col", None),
        P("row", "col"),
        P("row", "col"),
        P("row", "col"),
        P("row", "col", None),
        P(),
        P(),
        P(),
        P(),
        P(),
        P(),
    )
    return jax.shard_map(
        per_device, mesh=mesh, in_specs=placed, out_specs=P("row", "col", None), check_vma=False
    )
```

profile of v0, /device:TPU:8, one launch (start us, length us, event | category | flops | bytes accessed | tf_op | source)
XLA Modules:
  0.0 452.5 jit_solution(10674677785893327585)
XLA Ops:
  6.5 0.7 convert_element_type.41
  7.3 0.1 convert_element_type.42
  7.3 0.8 constant_dynamic-update-slice_fusion.4
  8.1 0.8 constant_dynamic-update-slice_fusion.3
  8.9 0.8 constant_dynamic-update-slice_fusion.2
  9.7 0.8 constant_dynamic-update-slice_fusion.1
  10.4 0.8 constant_dynamic-update-slice_fusion
  11.2 1.1 fusion.14
  12.3 0.3 fusion.23
  12.7 1.1 multiply_convert_fusion.5
  13.8 0.0 all-gather.5.cloned.1.call-start
  13.8 0.7 copy.80
  14.6 39.2 %all-gather.3.cloned.1.call-done = bf16[384,24,128]{2,1,0:T(8,128)(2,1)} async-done(((bf16[24,24,128]{2,1,0:T(8,128)(2,1)}), bf16[384,24,128]{2,1,0:T(8,128)(2,1)}) %all-gather.3.cloned.1.call-update) | async-done | bytes 2359312 | tf_op jit(solution)/shard_map/all_gather | solution.py:16
  53.8 9.6 %all-to-all-start = ((bf16[384,24,128]{2,1,0:T(8,128)(2,1)}), bf16[384,24,128]{2,1,0:T(8,128)(2,1)}, u32[]{:S(2)}, u32[]{:S(2)}) async-start(bf16[384,24,128]{2,1,0:T(8,128)(2,1)} %all-gather.3.cloned.1.call-done), calls=%async_computation | async-start | bytes 4718592 | tf_op jit(solution)/shard_map/all_to_all | solution.py:21
  63.5 0.3 fusion.21
  63.8 0.1 div.37
  63.9 82.3 %all-gather.5.cloned.1.call-done = bf16[24,384,128]{2,0,1:T(8,128)(2,1)} async-done(((bf16[24,24,128]{2,0,1:T(8,128)(2,1)}), bf16[24,384,128]{2,0,1:T(8,128)(2,1)}) %all-gather.5.cloned.1.call-update) | async-done | bytes 2359312 | tf_op jit(solution)/shard_map/all_gather | solution.py:66
  146.2 3.7 copy.82
  149.9 3.8 copy.79
  153.7 4.5 copy.90
  158.2 3.9 bitcast_reduce_fusion
  162.1 0.1 copy.85
  162.2 1.9 copy.83
  164.0 0.3 multiply_reduce_fusion.2
  164.3 0.1 copy.103
  164.4 0.1 copy.87
  164.5 0.3 multiply_reduce_fusion.1
  164.8 0.1 copy.104
  164.9 0.1 copy.89
  164.9 1.0 fusion.16
  166.0 0.4 copy.95
  166.4 4.8 %convolution_bitcast_fusion.1 = f32[24,384,128]{1,0,2:T(8,128)} fusion(bf16[24,384,128]{1,0,2:T(8,128)(2,1)} %copy.90, bf16[24,24,128]{0,1,2:T(8,128)(2,1)S(1)} %copy.95), kind=kOutput, calls=%fused_computation.1 | convolution fusion | flops 56623104 | bytes 7225344 | tf_op jit(solution)/shard_map/ijh,jkh->ikh/dot_general | solution.py:84
  171.3 6.1 %copy.92 = f32[24,384,128]{2,0,1:T(8,128)} copy(f32[24,384,128]{1,0,2:T(8,128)} %convolution_bitcast_fusion.1) | data formatting | bytes 9437184 | tf_op jit(solution)/shard_map/ijh,jkh->ikh/transpose | solution.py:84
  177.4 3.1 convolution_bitcast_fusion
  180.5 6.1 %copy.96 = f32[24,384,128]{2,0,1:T(8,128)} copy(f32[24,384,128]{1,0,2:T(8,128)} %convolution_bitcast_fusion) | data formatting | bytes 9437184 | tf_op jit(solution)/shard_map/ijh,ikh->jkh/transpose | solution.py:25
  186.6 146.0 %all_to_all.36 = f32[24,384,128]{2,0,1:T(8,128)S(1)} all-to-all(f32[24,384,128]{2,0,1:T(8,128)} %copy.96), channel_id=1, replica_groups=mesh['row'=16,'col'=16] {'col'}, dimensions={1} | all-to-all | bytes 9437184 | tf_op jit(solution)/shard_map/all_to_all | solution.py:28
  332.6 3.0 copy.98
  335.6 34.8 %reduce-scatter.3.cloned.1.call-done = f32[24,24,128]{2,0,1:T(8,128)} async-done(((f32[24,384,128]{2,0,1:T(8,128)}), f32[24,24,128]{2,0,1:T(8,128)}) %reduce-scatter.3.cloned.1.call-update) | async-done | bytes 294928 | tf_op jit(solution)/shard_map/reduce_scatter | solution.py:87
  370.4 1.0 copy.93
  371.4 70.7 %reduce-scatter.5.cloned.1.call-done = f32[24,24,128]{2,1,0:T(8,128)} async-done(((f32[384,24,128]{2,1,0:T(8,128)}), f32[24,24,128]{2,1,0:T(8,128)}) %reduce-scatter.5.cloned.1.call-update) | async-done | bytes 294928 | tf_op jit(solution)/shard_map/reduce_scatter | solution.py:29
  442.1 1.2 multiply_convert_fusion
  443.6 0.2 fusion.3
  443.8 0.5 fusion.22
  444.3 0.1 div.40
  444.4 0.3 multiply_reduce_fusion
  444.7 0.1 copy.99
  444.8 0.1 copy.100
  444.9 1.1 subtract_multiply_fusion
  (36 shorter events, 0.4 us)
Async XLA Ops:
  6.5 56.9 %copy-start = (bf16[128,128]{1,0:T(8,128)(2,1)S(1)}, bf16[128,128]{1,0:T(8,128)(2,1)}, u32[]{:S(2)}) copy-start(bf16[128,128]{1,0:T(8,128)(2,1)} %param.21) | copy-start | bytes 98308
  6.5 47.3 %all-gather.3.cloned.1.call-start = ((), (), s32[]{:S(2)}) async-start(), calls=%async_computation.4 | async-start | bytes 2506752 | tf_op jit(solution)/shard_map/all_gather | solution.py:16
  12.7 50.8 %copy-start.1 = (f32[576,640]{1,0:T(8,128)}, f32[576,640]{1,0:T(8,128)S(1)}, u32[]{:S(2)}) copy-start(f32[576,640]{1,0:T(8,128)S(1)} %fusion.23) | copy-start | bytes 4423684
  13.8 132.4 %all-gather.5.cloned.1.call-start = ((), (), s32[]{:S(2)}) async-start(), calls=%async_computation.5 | async-start | bytes 2506752 | tf_op jit(solution)/shard_map/all_gather | solution.py:66
  14.5 48.9 %copy-start.7 = (bf16[24,24,128]{2,1,0:T(8,128)(2,1)S(1)}, bf16[24,24,128]{2,1,0:T(8,128)(2,1)}, u32[]{:S(2)}) copy-start(bf16[24,24,128]{2,1,0:T(8,128)(2,1)} %param.15) | copy-start | bytes 442372
  53.8 96.1 %all-to-all-start = ((bf16[384,24,128]{2,1,0:T(8,128)(2,1)}), bf16[384,24,128]{2,1,0:T(8,128)(2,1)}, u32[]{:S(2)}, u32[]{:S(2)}) async-start(bf16[384,24,128]{2,1,0:T(8,128)(2,1)} %all-gather.3.cloned.1.call-done), calls=%async_computation | async-start | bytes 4718592 | tf_op jit(solution)/shard_map/all_to_all | solution.py:21
  63.4 307.0 %reduce-scatter.3.cloned.1.call-start = ((), (), s32[]{:S(2)}) async-start(), calls=%async_computation.6 | async-start | bytes 5013504 | tf_op jit(solution)/shard_map/reduce_scatter | solution.py:87
  177.3 264.8 %reduce-scatter.5.cloned.1.call-start = ((), (), s32[]{:S(2)}) async-start(), calls=%async_computation.7 | async-start | bytes 5013504 | tf_op jit(solution)/shard_map/reduce_scatter | solution.py:29
  335.6 106.5 %copy-start.2 = (f32[576,640]{1,0:T(8,128)S(1)}, f32[576,640]{1,0:T(8,128)}, u32[]{:S(2)}) copy-start(f32[576,640]{1,0:T(8,128)} %copy-done.1) | copy-start | bytes 4423684
  335.6 108.0 %copy-start.4 = (bf16[24,24,128]{2,1,0:T(8,128)(2,1)S(1)}, bf16[24,24,128]{2,1,0:T(8,128)(2,1)}, u32[]{:S(2)}) copy-start(bf16[24,24,128]{2,1,0:T(8,128)(2,1)} %get-tuple-element.13) | copy-start | bytes 442372
  335.6 108.0 %copy-start.8 = (bf16[24,24,128]{2,1,0:T(8,128)(2,1)S(1)}, bf16[24,24,128]{2,1,0:T(8,128)(2,1)}, u32[]{:S(2)}) copy-start(bf16[24,24,128]{2,1,0:T(8,128)(2,1)} %param.15) | copy-start | bytes 442372
  443.4 1.0 copy-start.3
  443.4 1.0 copy-start.5
  443.4 1.0 copy-start.6
Sparse Core Ops, SparseCore 0:
  13.9 39.8 all-gather.2
  56.2 89.9 all-gather.4
  177.5 192.8 reduce-scatter.2
  372.8 69.2 reduce-scatter.4
where the time goes:
time: 454 us; the launch traced here: 453 us
  waiting for transfers between devices  227 us (50%)
  blocking collectives  146 us (32%)
  local copies, waits for them, and re-layouts  35.9 us (8%)
  between operations  13.4 us (3%)
  matrix products  13.2 us (3%)
  starting transfers between devices  9.72 us (2%)
  other arithmetic  7.22 us (2%)
    all_to_all x1, blocking collectives, panel_grad_right(): lax.all_to_all(partial_right, 'col', split_axis=1, concat_axis=0, tiled=T...  146 us
    all_gather x1, waiting for transfers between devices, per_device(): left_rows = lax.all_gather(left_edge, 'col', axis=1, tiled=True)  82.3 us
    reduce_scatter x1, waiting for transfers between devices, panel_grad_right(): return lax.psum_scatter(moved_right, 'row', scatter_dimension=0, tiled=True)  70.7 us
    all_gather x1, waiting for transfers between devices, column_panel(): return lax.all_gather(right_edge, 'row', axis=0, tiled=True)  39.2 us
    reduce_scatter x1, waiting for transfers between devices, per_device(): lax.psum_scatter(partial_left, 'col', scatter_dimension=1, tiled=True)  34.8 us
    all_to_all x1, starting transfers between devices, panel_right(): lax.all_to_all(right_cols, 'col', split_axis=0, concat_axis=1, tiled=True)  9.59 us
  transfers between devices with their start and end apart: 5, of which 4 were waited for; matrix products, arithmetic and copies ran while one was open for 4% of the time, Pallas kernels for 0%

commit v1 on v0

--- a/solution.py
+++ b/solution.py
@@ -13,7 +13,9 @@
 
 
 def column_panel(right_edge):
-    return lax.all_gather(right_edge, "row", axis=0, tiled=True)
+    return jnp.concatenate(
+        lax.all_to_all(jnp.stack([right_edge] * lax.axis_size("row")), "row", 0, 0), axis=0
+    )
 
 
 def panel_right(right_edge):

time: 454 us -> 432 us (0.952)
  waiting for transfers between devices: 227 us -> 198 us
  starting transfers between devices: 9.72 us -> 16.7 us
    all_gather x1 -> x0, waiting for transfers between devices: 39.2 us -> none  [column_panel(): return lax.all_gather(right_edge, 'row', axis=0, tiled=True)]
    all_to_all x0 -> x1, waiting for transfers between devices: none -> 35.6 us  [column_panel(): lax.all_to_all(jnp.stack([right_edge] * lax.axis_size('row')), 'row', 0, 0)]
    all_gather x1, waiting for transfers between devices: 82.3 us -> 48.1 us  [per_device(): left_rows = lax.all_gather(left_edge, 'col', axis=1, tiled=True)]
    all_to_all x1, waiting for transfers between devices: 0.01 us -> 19.8 us  [panel_right(): lax.all_to_all(right_cols, 'col', split_axis=0, concat_axis=1, tiled=True)]
    reduce_scatter x1, waiting for transfers between devices: 34.8 us -> 23.5 us  [per_device(): lax.psum_scatter(partial_left, 'col', scatter_dimension=1, tiled=True)]
    all_to_all x0 -> x1, starting transfers between devices: none -> 5.8 us  [column_panel(): lax.all_to_all(jnp.stack([right_edge] * lax.axis_size('row')), 'row', 0, 0)]
  transfers between devices with their start and end apart: 5 -> 5, of which waited for: 4 -> 5; matrix products, arithmetic and copies ran while one was open for 4% -> 4% of each run, Pallas kernels for 0% -> 0%
where the time goes in v1:
time: 432 us; the launch traced here: 431 us
  waiting for transfers between devices  198 us (46%)
  blocking collectives  146 us (34%)
  local copies, waits for them, and re-layouts  37.7 us (9%)
  starting transfers between devices  16.7 us (4%)
  between operations  13.4 us (3%)
  matrix products  13.2 us (3%)
  other arithmetic  6.35 us (1%)
    all_to_all x1, blocking collectives, panel_grad_right(): lax.all_to_all(partial_right, 'col', split_axis=1, concat_axis=0, tiled=T...  146 us
    reduce_scatter x1, waiting for transfers between devices, panel_grad_right(): return lax.psum_scatter(moved_right, 'row', scatter_dimension=0, tiled=True)  70.8 us
    all_gather x1, waiting for transfers between devices, per_device(): left_rows = lax.all_gather(left_edge, 'col', axis=1, tiled=True)  48.1 us
    all_to_all x1, waiting for transfers between devices, column_panel(): lax.all_to_all(jnp.stack([right_edge] * lax.axis_size('row')), 'row', 0, 0)  35.6 us
    reduce_scatter x1, waiting for transfers between devices, per_device(): lax.psum_scatter(partial_left, 'col', scatter_dimension=1, tiled=True)  23.5 us
    all_to_all x1, waiting for transfers between devices, panel_right(): lax.all_to_all(right_cols, 'col', split_axis=0, concat_axis=1, tiled=True)  19.8 us
    all_to_all x1, starting transfers between devices, panel_right(): lax.all_to_all(right_cols, 'col', split_axis=0, concat_axis=1, tiled=True)  10.8 us
  transfers between devices with their start and end apart: 5, of which 5 were waited for; matrix products, arithmetic and copies ran while one was open for 4% of the time, Pallas kernels for 0%

profile of v1, /device:TPU:8, one launch (start us, length us, event | category | flops | bytes accessed | tf_op | source)
XLA Modules:
  0.0 431.3 jit_solution(156978451513321441)
XLA Ops:
  6.5 0.7 convert_element_type.41
  7.3 0.1 convert_element_type.42
  7.3 0.8 constant_dynamic-update-slice_fusion.4
  8.1 0.8 constant_dynamic-update-slice_fusion.3
  8.9 0.8 constant_dynamic-update-slice_fusion.2
  9.6 0.8 constant_dynamic-update-slice_fusion.1
  10.4 0.8 constant_dynamic-update-slice_fusion
  11.2 1.1 fusion.14
  12.3 0.3 fusion.23
  12.7 0.2 multiply_convert_fusion.5
  12.9 1.9 stack.3
  14.7 5.8 %all-to-all-start = ((bf16[16,24,24,128]{3,2,1,0:T(8,128)(2,1)}), bf16[16,24,24,128]{3,2,1,0:T(8,128)(2,1)}, u32[]{:S(2)}, u32[]{:S(2)}) async-start(bf16[16,24,24,128]{3,2,1,0:T(8,128)(2,1)} %stack.3), calls=%async_computation | async-start | bytes 4718592 | tf_op jit(solution)/shard_map/all_to_all | solution.py:17
  20.6 0.7 copy.80
  21.3 35.6 %all-to-all-done = bf16[16,24,24,128]{3,2,1,0:T(8,128)(2,1)} async-done(((bf16[16,24,24,128]{3,2,1,0:T(8,128)(2,1)}), bf16[16,24,24,128]{3,2,1,0:T(8,128)(2,1)}, u32[]{:S(2)}, u32[]{:S(2)}) %all-to-all-start) | async-done | bytes 2359328 | tf_op jit(solution)/shard_map/all_to_all | solution.py:17
  56.9 10.8 %all-to-all-start.1 = ((bf16[384,24,128]{2,1,0:T(8,128)(2,1)}), bf16[384,24,128]{2,1,0:T(8,128)(2,1)}, u32[]{:S(2)}, u32[]{:S(2)}) async-start(bf16[384,24,128]{2,1,0:T(8,128)(2,1)} %bitcast.2), calls=%async_computation.1 | async-start | bytes 4718592 | tf_op jit(solution)/shard_map/all_to_all | solution.py:23
  67.8 0.3 fusion.21
  68.1 0.1 div.37
  68.2 48.1 %all-gather.2.cloned.1.call-done = bf16[24,384,128]{2,0,1:T(8,128)(2,1)} async-done(((bf16[24,24,128]{2,0,1:T(8,128)(2,1)}), bf16[24,384,128]{2,0,1:T(8,128)(2,1)}) %all-gather.2.cloned.1.call-update) | async-done | bytes 2359312 | tf_op jit(solution)/shard_map/all_gather | solution.py:68
  116.3 3.7 copy.82
  120.0 19.8 %all-to-all-done.1 = bf16[384,24,128]{2,1,0:T(8,128)(2,1)} async-done(((bf16[384,24,128]{2,1,0:T(8,128)(2,1)}), bf16[384,24,128]{2,1,0:T(8,128)(2,1)}, u32[]{:S(2)}, u32[]{:S(2)}) %all-to-all-start.1) | async-done | bytes 2359328 | tf_op jit(solution)/shard_map/all_to_all | solution.py:23
  139.8 3.8 copy.79
  143.6 4.5 %copy.90 = bf16[24,384,128]{1,0,2:T(8,128)(2,1)} copy(bf16[24,384,128]{2,1,0:T(8,128)(2,1)} %bitcast.62) | data formatting | bytes 4718592 | tf_op jit(solution)/shard_map/all_to_all | solution.py:23
  148.1 3.9 bitcast_reduce_fusion
  152.0 0.1 copy.85
  152.1 1.9 copy.83
  154.0 0.3 multiply_reduce_fusion.2
  154.3 0.1 copy.87
  154.4 0.3 multiply_reduce_fusion.1
  154.7 0.1 copy.104
  154.8 0.1 copy.89
  154.9 1.0 fusion.16
  155.9 0.4 copy.95
  156.3 4.9 %convolution_bitcast_fusion.1 = f32[24,384,128]{1,0,2:T(8,128)} fusion(bf16[24,384,128]{1,0,2:T(8,128)(2,1)} %copy.90, bf16[24,24,128]{0,1,2:T(8,128)(2,1)S(1)} %copy.95), kind=kOutput, calls=%fused_computation.1 | convolution fusion | flops 56623104 | bytes 7225344 | tf_op jit(solution)/shard_map/ijh,jkh->ikh/dot_general | solution.py:86
  161.2 6.0 %copy.92 = f32[24,384,128]{2,0,1:T(8,128)} copy(f32[24,384,128]{1,0,2:T(8,128)} %convolution_bitcast_fusion.1) | data formatting | bytes 9437184 | tf_op jit(solution)/shard_map/ijh,jkh->ikh/transpose | solution.py:86
  167.3 3.1 convolution_bitcast_fusion
  170.4 6.1 %copy.96 = f32[24,384,128]{2,0,1:T(8,128)} copy(f32[24,384,128]{1,0,2:T(8,128)} %convolution_bitcast_fusion) | data formatting | bytes 9437184 | tf_op jit(solution)/shard_map/ijh,ikh->jkh/transpose | solution.py:27
  176.5 146.0 %all_to_all.41 = f32[24,384,128]{2,0,1:T(8,128)S(1)} all-to-all(f32[24,384,128]{2,0,1:T(8,128)} %copy.96), channel_id=1, replica_groups=mesh['row'=16,'col'=16] {'col'}, dimensions={1} | all-to-all | bytes 9437184 | tf_op jit(solution)/shard_map/all_to_all | solution.py:30
  322.6 3.0 copy.98
  325.6 23.5 %reduce-scatter.3.cloned.1.call-done = f32[24,24,128]{2,0,1:T(8,128)} async-done(((f32[24,384,128]{2,0,1:T(8,128)}), f32[24,24,128]{2,0,1:T(8,128)}) %reduce-scatter.3.cloned.1.call-update) | async-done | bytes 294928 | tf_op jit(solution)/shard_map/reduce_scatter | solution.py:89
  349.1 1.0 copy.93
  350.1 70.8 %reduce-scatter.5.cloned.1.call-done = f32[24,24,128]{2,1,0:T(8,128)} async-done(((f32[384,24,128]{2,1,0:T(8,128)}), f32[24,24,128]{2,1,0:T(8,128)}) %reduce-scatter.5.cloned.1.call-update) | async-done | bytes 294928 | tf_op jit(solution)/shard_map/reduce_scatter | solution.py:31
  420.9 1.2 multiply_convert_fusion
  422.4 0.2 fusion.3
  422.6 0.5 fusion.22
  423.1 0.1 div.40
  423.2 0.3 multiply_reduce_fusion
  423.6 0.1 copy.100
  423.7 1.1 subtract_multiply_fusion
  (36 shorter events, 0.5 us)
Async XLA Ops:
  6.5 61.2 %copy-start = (bf16[128,128]{1,0:T(8,128)(2,1)S(1)}, bf16[128,128]{1,0:T(8,128)(2,1)}, u32[]{:S(2)}) copy-start(bf16[128,128]{1,0:T(8,128)(2,1)} %param.21) | copy-start | bytes 98308
  12.7 55.1 %copy-start.1 = (f32[576,640]{1,0:T(8,128)}, f32[576,640]{1,0:T(8,128)S(1)}, u32[]{:S(2)}) copy-start(f32[576,640]{1,0:T(8,128)S(1)} %fusion.23) | copy-start | bytes 4423684
  14.7 42.2 %all-to-all-start = ((bf16[16,24,24,128]{3,2,1,0:T(8,128)(2,1)}), bf16[16,24,24,128]{3,2,1,0:T(8,128)(2,1)}, u32[]{:S(2)}, u32[]{:S(2)}) async-start(bf16[16,24,24,128]{3,2,1,0:T(8,128)(2,1)} %stack.3), calls=%async_computation | async-start | bytes 4718592 | tf_op jit(solution)/shard_map/all_to_all | solution.py:17
  20.5 95.8 %all-gather.2.cloned.1.call-start = ((), (), s32[]{:S(2)}) async-start(), calls=%async_computation.5 | async-start | bytes 2506752 | tf_op jit(solution)/shard_map/all_gather | solution.py:68
  56.9 10.9 %copy-start.7 = (bf16[24,24,128]{2,1,0:T(8,128)(2,1)S(1)}, bf16[24,24,128]{2,1,0:T(8,128)(2,1)}, u32[]{:S(2)}) copy-start(bf16[24,24,128]{2,1,0:T(8,128)(2,1)} %param.15) | copy-start | bytes 442372
  56.9 82.9 %all-to-all-start.1 = ((bf16[384,24,128]{2,1,0:T(8,128)(2,1)}), bf16[384,24,128]{2,1,0:T(8,128)(2,1)}, u32[]{:S(2)}, u32[]{:S(2)}) async-start(bf16[384,24,128]{2,1,0:T(8,128)(2,1)} %bitcast.2), calls=%async_computation.1 | async-start | bytes 4718592 | tf_op jit(solution)/shard_map/all_to_all | solution.py:23
  67.7 281.4 %reduce-scatter.3.cloned.1.call-start = ((), (), s32[]{:S(2)}) async-start(), calls=%async_computation.6 | async-start | bytes 5013504 | tf_op jit(solution)/shard_map/reduce_scatter | solution.py:89
  167.3 253.7 %reduce-scatter.5.cloned.1.call-start = ((), (), s32[]{:S(2)}) async-start(), calls=%async_computation.7 | async-start | bytes 5013504 | tf_op jit(solution)/shard_map/reduce_scatter | solution.py:31
  325.6 95.4 %copy-start.2 = (f32[576,640]{1,0:T(8,128)S(1)}, f32[576,640]{1,0:T(8,128)}, u32[]{:S(2)}) copy-start(f32[576,640]{1,0:T(8,128)} %copy-done.1) | copy-start | bytes 4423684
  325.6 96.8 %copy-start.4 = (bf16[24,24,128]{2,1,0:T(8,128)(2,1)S(1)}, bf16[24,24,128]{2,1,0:T(8,128)(2,1)}, u32[]{:S(2)}) copy-start(bf16[24,24,128]{2,1,0:T(8,128)(2,1)} %get-tuple-element.13) | copy-start | bytes 442372
  325.6 96.8 %copy-start.8 = (bf16[24,24,128]{2,1,0:T(8,128)(2,1)S(1)}, bf16[24,24,128]{2,1,0:T(8,128)(2,1)}, u32[]{:S(2)}) copy-start(bf16[24,24,128]{2,1,0:T(8,128)(2,1)} %param.15) | copy-start | bytes 442372
  422.2 1.0 copy-start.3
  422.2 1.0 copy-start.5
  422.2 1.0 copy-start.6
Sparse Core Ops, SparseCore 0:
  23.8 92.4 all-gather.1
  167.4 181.6 reduce-scatter.2
  351.6 69.2 reduce-scatter.4
